TPU v7x, 32 devices: a whole 2x2x4 slice. The times are simulated.
32 devices in a mesh: parts: 2 (over y), wide: 4 (over z), col: 2 (over x), pair: 2 (over core).
Axes of the slice: x: 2, y: 2, z: 4, core: 2. Of those that a mesh axis runs over, the one named last changes fastest.
Arguments:
- peram: bfloat16 [32, 384, 2, 384], P(('parts', 'wide'), ('col', 'pair')), parts along dimension 0, may hold values from -0.21875 to 0.21875
- elements: bfloat16 [8, 384, 2, 384], P('parts'), parts along dimension 0, may hold values from -6 to 6
- l1_peram: int32 [8, 4], P(('parts', 'wide')), parts along dimension 0, may hold values from 0 to 3
- l1_elem: int32 [8, 4], P(('parts', 'wide')), parts along dimension 0, may hold values from 0 to 3
- owners: int32 [8, 4], P(('parts', 'wide')), parts along dimension 0, may hold values from 0 to 1, as said below
- first_ops: int32 [8, 2, 4], P('parts', 'col'), parts along dimension 0, may hold values from 0 to 11, as said below
- second_ops: int32 [8, 2, 4], P(('parts', 'wide'), 'col'), parts along dimension 0, may hold values from 0 to 2, as said below
- product_ops: int32 [8, 2, 4, 2], P(('parts', 'wide'), 'col'), parts along dimension 0, may hold values from 0 to 3
- weights: int32 [16, 32], P('parts', ('wide', 'col')), parts along dimension 0, may hold values from -3 to 3
Outputs:
- products: bfloat16 [64, 2, 2, 96, 2, 384], P(('parts', 'wide', 'col'), None, 'pair'), parts along dimension 0
- diagrams: float32 [16, 2], P('parts'), parts along dimension 0
There are 2 independent parts, one for each index of `parts`. A program takes and returns all parts, laid end to end along the dimension named above; each array names one. Nothing has to cross between parts.
Inputs may be any that keep to these rules, and one draw needn't show every extreme that they name: `owners`: in every wide group each col index owns 1 to 3 blocks, and some col index owns exactly 3. `first_ops`: for owner (g, c) an entry s * 3 + k names the k-th block of group s owned by col index c, k below the number of such blocks. At most 2 tasks of one owner name one group s, exactly 2 for some s of every owner, and tasks of one owner that name the same group name the same block. `second_ops`: entries of owner (g, c) are below the number of blocks of group g owned by col index c.
All inputs are finite; a program needn't handle non-finite values.
Results may differ from a plain program's by a relative error of at most 0.0082.
Values may be sent and summed in bfloat16 or wider, within the bound.
A program may use at most 128 MiB of HBM per device.

v0:
```python
import math

import jax
import jax.numpy as jnp
from jax import lax
from jax.sharding import PartitionSpec as P

CAP_LANE = 3
CAP_PEER = 2


def partner(value, axis, stride):
    mask = 2**stride
    pairs = [(source, source ^ mask) for source in range(lax.axis_size(axis))]
    return lax.ppermute(value, axis, pairs)


def complex_rows(left, right, factor):
    left_real = left[:, 0, :]
    left_imag = left[:, 1, :]
    right_real = right[:, 0, :]
    right_imag = right[:, 1, :]
    real_part = jnp.dot(left_real, right_real, preferred_element_type=jnp.float32) - jnp.dot(
        left_imag, right_imag, preferred_element_type=jnp.float32
    )
    imag_part = jnp.dot(left_real, right_imag, preferred_element_type=jnp.float32) + jnp.dot(
        left_imag, right_real, preferred_element_type=jnp.float32
    )
    return jnp.stack([real_part, imag_part], axis=1) * factor


def one_hot_rows(values, width):
    return (values[..., None] == jnp.arange(width, dtype=jnp.int32)).astype(jnp.float32)


def shards(peram, elements, l1_peram, l1_elem, owners, first_ops, second_ops, product_ops, weights):
    nvec = elements.shape[1]
    nelem = elements.shape[0]
    nperam = peram.shape[0]
    rows_dev = peram.shape[1]
    lanes = lax.axis_size("col")
    rows_half = lanes * rows_dev
    pair_index = lax.axis_index("pair")
    factor = 1.0 / math.sqrt(2.0 * nvec)

    def whole_rows(own_half, partner_half):
        leading = own_half.shape[:-3]
        shaped_own = own_half.reshape(leading + (lanes, rows_dev, 2, nvec))
        shaped_partner = partner_half.reshape(leading + (lanes, rows_dev, 2, nvec))
        lower = jnp.where(pair_index == 0, shaped_own, shaped_partner)
        upper = jnp.where(pair_index == 0, shaped_partner, shaped_own)
        return jnp.stack([lower, upper], axis=len(leading) + 1).reshape(leading + (nvec, 2, nvec))

    peram_rows = peram.reshape(nperam * rows_dev, 2, nvec)
    combos = jax.vmap(lambda element: complex_rows(peram_rows, element, 1.0))(elements)
    combos = combos.astype(jnp.bfloat16).reshape(nelem * nperam, rows_dev * 2 * nvec)
    owner_row = owners[0]
    lane_hot = (owner_row[:, None] == jnp.arange(lanes, dtype=jnp.int32)[None, :]).astype(jnp.int32)
    lane_rank = jnp.sum((jnp.cumsum(lane_hot, axis=0) - lane_hot) * lane_hot, axis=1)
    slot_rows = owner_row * CAP_LANE + lane_rank
    combo_ids = l1_elem[0] * nperam + l1_peram[0]
    pick_blocks = jnp.dot(
        one_hot_rows(slot_rows, lanes * CAP_LANE).T, one_hot_rows(combo_ids, nelem * nperam)
    )
    outgoing = jnp.dot(
        pick_blocks.astype(jnp.bfloat16), combos, preferred_element_type=jnp.float32
    ).astype(jnp.bfloat16)
    outgoing = outgoing.reshape(lanes, CAP_LANE, rows_dev, 2, nvec)
    arrived = lax.all_to_all(outgoing, "col", split_axis=0, concat_axis=2, tiled=True)[0]
    resident = whole_rows(arrived, partner(arrived, "pair", 0))
    here = lax.axis_index("wide")
    peers = lax.axis_size("wide")
    first_ids = first_ops[:, 0, :]
    tasks = first_ids.shape[1]
    sources = first_ids // CAP_LANE
    slot_rank = first_ids % CAP_LANE
    task_range = jnp.arange(tasks, dtype=jnp.int32)
    same_source = (sources[:, :, None] == sources[:, None, :]) & (
        task_range[None, None, :] < task_range[None, :, None]
    )
    repeat_rank = jnp.sum(same_source.astype(jnp.int32), axis=2)
    from_here = (sources == here).astype(jnp.float32)
    rank_hot = one_hot_rows(slot_rank, CAP_LANE)
    arrived_flat = arrived.reshape(CAP_LANE, rows_half * 2 * nvec)
    my_sources = lax.dynamic_index_in_dim(sources, here, 0, keepdims=False)
    slot_ids = jnp.arange(peers, dtype=jnp.int32)[:, None] * CAP_PEER + repeat_rank
    pick_send = jnp.einsum(
        "wts,wtr->sr", one_hot_rows(slot_ids, peers * CAP_PEER) * from_here[:, :, None], rank_hot
    )
    outgoing_first = jnp.dot(
        pick_send.astype(jnp.bfloat16), arrived_flat, preferred_element_type=jnp.float32
    ).astype(jnp.bfloat16)
    outgoing_first = outgoing_first.reshape(peers, CAP_PEER, rows_half, 2, nvec)
    pool = lax.all_to_all(outgoing_first, "wide", split_axis=0, concat_axis=0, tiled=True).reshape(
        peers * CAP_PEER, rows_half, 2, nvec
    )
    my_repeat = lax.dynamic_index_in_dim(repeat_rank, here, 0, keepdims=False)
    pool_index = my_sources * CAP_PEER + my_repeat
    second_slots = second_ops[0, 0]

    def one_task(indices):
        pool_slot, resident_slot = indices
        return complex_rows(pool[pool_slot], resident[resident_slot], factor).astype(jnp.bfloat16)

    level_two = lax.map(one_task, (pool_index, second_slots))
    pairs = product_ops[0, 0]
    partner_products = partner(level_two, "pair", 0)
    whole_products = whole_rows(level_two, partner_products)
    right_ops = jnp.take(whole_products, pairs[:, 1], axis=0)
    left_ops = jnp.take(level_two, pairs[:, 0], axis=0)
    local_rows = jnp.arange(rows_half, dtype=jnp.int32)
    global_rows = (
        local_rows // rows_dev * lax.axis_size("pair") + pair_index
    ) * rows_dev + local_rows % rows_dev
    diag_mask = (jnp.arange(nvec, dtype=jnp.int32)[None, :] == global_rows[:, None]).astype(
        jnp.float32
    )

    def one_product(operands):
        left_block, right_block = operands
        full_block = complex_rows(left_block, right_block, factor)
        block_traces = jnp.sum(full_block * diag_mask[:, None, :], axis=(0, 2))
        return (full_block.astype(jnp.bfloat16), block_traces)

    products, traces = lax.map(one_product, (left_ops, right_ops))
    partial_sums = (
        jnp.dot(weights.astype(jnp.float32), traces, precision=lax.Precision.HIGHEST) / nvec
    )
    diagrams = lax.psum(partial_sums, ("wide", "col", "pair"))
    return (products.reshape(products.shape[0], lanes, 1, rows_dev, 2, nvec), diagrams)


def solution(mesh):
    placed = (
        P(("parts", "wide"), ("col", "pair"), None, None),
        P("parts", None, None, None),
        P(("parts", "wide"), None),
        P(("parts", "wide"), None),
        P(("parts", "wide"), None),
        P("parts", "col", None),
        P(("parts", "wide"), "col", None),
        P(("parts", "wide"), "col", None, None),
        P("parts", ("wide", "col")),
    )
    return jax.shard_map(
        shards,
        mesh=mesh,
        in_specs=placed,
        out_specs=(P(("parts", "wide", "col"), None, "pair", None, None, None), P("parts", None)),
        check_vma=False,
    )
```

profile of v0, /device:TPU:0, one launch (start us, length us, event | category | flops | bytes accessed | tf_op | source)
XLA Modules:
  0.0 192.2 jit_solution(14367576414557641374)
XLA Ops:
  0.6 1.1 copy.43
  1.8 6.5 %fusion.45 = (bf16[4,384,1,384]{3,2,1,0:T(2,128)(2,1)S(1)}, bf16[4,384,1,384]{3,2,1,0:T(2,128)(2,1)S(1)}) fusion(bf16[4,384,2,384]{3,2,1,0:T(2,128)(2,1)} %param.14), kind=kLoop, calls=%fused_computation.113 | loop fusion | bytes 4718592 | tf_op jit(solution)/shard_map/vmap()/slice | solution.py:21
  11.7 3.8 %copy.46 = bf16[4,384,2,384]{3,2,1,0:T(2,128)(2,1)} copy(bf16[4,384,2,384]{3,1,0,2:T(8,128)(2,1)S(1)} %maximum_bitcast_fusion) | data formatting | bytes 4718592 | tf_op jit(solution)/shard_map/convert_element_type | solution.py:56
  15.6 3.1 %reshape.310 = bf16[16,73728]{1,0:T(8,128)(2,1)S(1)} reshape(bf16[4,384,2,384]{3,2,1,0:T(2,128)(2,1)} %copy.46) | data formatting | bytes 4718592 | tf_op jit(solution)/shard_map/reshape | solution.py:56
  19.6 1.2 reshape.311
  20.9 1.0 copy.47
  21.9 4.2 %all-to-all-start = ((bf16[2,3,96,2,384]{4,2,3,1,0:T(8,128)(2,1)}), bf16[2,3,96,2,384]{4,2,3,1,0:T(8,128)(2,1)S(1)}, u32[]{:S(2)}, u32[]{:S(2)}) async-start(bf16[2,3,96,2,384]{4,2,3,1,0:T(8,128)(2,1)} %copy.47), calls=%async_computation | async-start | bytes 1769472 | tf_op jit(solution)/shard_map/all_to_all | solution.py:69
  26.5 12.3 %all-to-all-done = bf16[2,3,96,2,384]{4,2,3,1,0:T(8,128)(2,1)S(1)} async-done(((bf16[2,3,96,2,384]{4,2,3,1,0:T(8,128)(2,1)}), bf16[2,3,96,2,384]{4,2,3,1,0:T(8,128)(2,1)S(1)}, u32[]{:S(2)}, u32[]{:S(2)}) %all-to-all-start) | async-done | bytes 884768 | tf_op jit(solution)/shard_map/all_to_all | solution.py:69
  40.8 1.6 reshape_squeeze.6
  42.4 2.3 %convolution_convert_fusion = bf16[8,147456]{1,0:T(8,128)(2,1)S(1)} fusion(bf16[3,147456]{1,0:T(4,128)(2,1)} %reshape_squeeze.6, s32[4,4]{1,0:T(4,128)S(1)} %add_select_fusion, bf16[4,4]{1,0:T(4,128)(2,1)S(1)} %get-tuple-element.109, s32[4,4]{1,0:T(4,128)S(1)} %broadcast_add_fusion), kind=kOutput, calls=%fused_computation.35 | convolution fusion | flops 8258608 | bytes 3244192 | tf_op jit(solution)/shard_map/dot_general | solution.py:90
  44.7 3.5 %reshape.312 = bf16[4,2,192,2,384]{4,3,2,1,0:T(2,128)(2,1)} reshape(bf16[8,147456]{1,0:T(8,128)(2,1)S(1)} %convolution_convert_fusion) | data formatting | bytes 4718592 | tf_op jit(solution)/shard_map/reshape | solution.py:93
  48.2 5.2 %all-to-all-start.1 = ((bf16[4,2,192,2,384]{4,3,2,1,0:T(2,128)(2,1)}), bf16[4,2,192,2,384]{4,3,2,1,0:T(2,128)(2,1)}, u32[]{:S(2)}, u32[]{:S(2)}) async-start(bf16[4,2,192,2,384]{4,3,2,1,0:T(2,128)(2,1)} %reshape.312), calls=%async_computation.1 | async-start | bytes 4718592 | tf_op jit(solution)/shard_map/all_to_all | solution.py:94
  53.5 2.5 %collective-permute-done = bf16[3,192,2,384]{3,1,2,0:T(8,128)(2,1)} collective-permute-done((bf16[3,192,2,384]{3,1,2,0:T(8,128)(2,1)S(1)}, bf16[3,192,2,384]{3,1,2,0:T(8,128)(2,1)}, u32[]{:S(2)}, u32[]{:S(2)}) %collective-permute-start) | collective-permute-done | bytes 884768 | tf_op jit(solution)/shard_map/ppermute | solution.py:15
  56.0 1.3 bitcast_select_fusion.1
  57.8 48.7 %all-to-all-done.1 = bf16[4,2,192,2,384]{4,3,2,1,0:T(2,128)(2,1)} async-done(((bf16[4,2,192,2,384]{4,3,2,1,0:T(2,128)(2,1)}), bf16[4,2,192,2,384]{4,3,2,1,0:T(2,128)(2,1)}, u32[]{:S(2)}, u32[]{:S(2)}) %all-to-all-start.1) | async-done | bytes 2359328 | tf_op jit(solution)/shard_map/all_to_all | solution.py:94
  106.5 3.5 %copy.50 = bf16[4,2,192,2,384]{4,2,3,1,0:T(8,128)(2,1)} copy(bf16[4,2,192,2,384]{4,3,2,1,0:T(2,128)(2,1)} %all-to-all-done.1) | data formatting | bytes 4718592 | tf_op jit(solution)/shard_map/all_to_all | solution.py:94
  110.0 28.9 %while.23 = (s32[]{:T(128)}, bf16[4,192,2,384]{3,1,2,0:T(8,128)(2,1)S(1)}, s32[4]{0:T(128)S(1)}, bf16[8,192,2,384]{3,1,2,0:T(8,128)(2,1)}, s32[4]{0:T(128)S(1)},...) while((s32[]{:T(128)}, ...), condition=%wide.region_4.5_spmd, body=%wide.region_3.4_spmd.sunk | while | flops 227082240 | bytes 6193357 | solution.py:105
  115.2 1.0 dynamic-slice_bitcast_fusion.9
  122.4 1.0 dynamic-slice_bitcast_fusion.9
  140.4 1.2 broadcast_select_fusion.1
  142.3 2.3 %gather_fusion.1 = bf16[4,384,2,384]{3,1,2,0:T(8,128)(2,1)} fusion(bf16[4,384,2,384]{3,1,2,0:T(8,128)(2,1)S(1)} %bitcast.191, s32[1024]{0:T(1024)S(1)} %get-tuple-element.127), kind=kCustom, calls=%fused_computation.1 | custom fusion | bytes 4718608 | tf_op jit(solution)/shard_map/jit(_take)/gather | solution.py:109
  144.6 2.0 %broadcast_select_fusion = bf16[4,384,2,384]{3,1,2,0:T(8,128)(2,1)S(1)} fusion(bf16[4,384,2,384]{3,1,2,0:T(8,128)(2,1)} %gather_fusion.1, pred[4]{0:T(512)(128)(4,1)S(1)} %copy-done.4), kind=kLoop, calls=%fused_computation.41 | loop fusion | flops 1179648 | bytes 4718596 | tf_op jit(solution)/shard_map/jit(_take)/select_n | solution.py:109
  146.7 14.0 %while.24 = (s32[]{:T(128)}, bf16[4,192,2,384]{3,2,1,0:T(2,128)(2,1)}, f32[4,2]{1,0:T(4,128)S(1)}, bf16[4,192,2,384]{3,1,2,0:T(8,128)(2,1)}, bf16[4,384,2,384]{3...) while((s32[]{:T(128)}, bf16[4,192,2,384]{3,2,1,0:T(2,128)(2,1)}, ...), condition=%wide.region_7.8_spmd.clone, body=%wide.region_5.7_spmd.clone.sunk | while | flops 227672064 | bytes 7964025 | solution.py:125
  146.7 1.0 dynamic-slice_bitcast_fusion.11
  149.1 1.0 copy_dynamic-update-slice_fusion.2
  150.2 1.0 dynamic-slice_bitcast_fusion.11
  152.6 1.0 copy_dynamic-update-slice_fusion.2
  153.7 1.0 dynamic-slice_bitcast_fusion.11
  156.1 1.0 copy_dynamic-update-slice_fusion.2
  157.2 1.0 dynamic-slice_bitcast_fusion.11
  159.6 1.0 copy_dynamic-update-slice_fusion.2
  160.8 31.4 %psum.7 = f32[8,2]{0,1:T(2,128)} all-reduce(f32[8,2]{0,1:T(2,128)S(1)} %fusion.16), channel_id=1, replica_groups=mesh['parts'=2,'wide'=4,'col'=2,'pair'=2] {'wide','col','pair'}, use_global_device_ids=true, to_apply=%region_8.9 | all-reduce | flops 16 | bytes 128 | tf_op jit(solution)/shard_map/psum | solution.py:129
  (131 shorter events, 26.1 us)
Async XLA Ops:
  15.6 3.1 %copy-start.8 = (s32[1,4]{1,0:T(1,128)S(1)}, s32[1,4]{1,0:T(1,128)}, u32[]{:S(2)}) copy-start(s32[1,4]{1,0:T(1,128)} %param.17) | copy-start | bytes 52
  15.6 3.3 %copy-start.9 = (s32[1,4]{1,0:T(1,128)S(1)}, s32[1,4]{1,0:T(1,128)}, u32[]{:S(2)}) copy-start(s32[1,4]{1,0:T(1,128)} %param.15) | copy-start | bytes 52
  15.6 3.3 %copy-start.10 = (s32[1,4]{1,0:T(1,128)S(1)}, s32[1,4]{1,0:T(1,128)}, u32[]{:S(2)}) copy-start(s32[1,4]{1,0:T(1,128)} %param.16) | copy-start | bytes 52
  20.9 5.3 %copy-start.2 = (s32[4,1,4]{2,1,0:T(1,128)S(1)}, s32[4,1,4]{2,1,0:T(1,128)}, u32[]{:S(2)}) copy-start(s32[4,1,4]{2,1,0:T(1,128)} %param.18) | copy-start | bytes 196
  21.9 16.9 %all-to-all-start = ((bf16[2,3,96,2,384]{4,2,3,1,0:T(8,128)(2,1)}), bf16[2,3,96,2,384]{4,2,3,1,0:T(8,128)(2,1)S(1)}, u32[]{:S(2)}, u32[]{:S(2)}) async-start(bf16[2,3,96,2,384]{4,2,3,1,0:T(8,128)(2,1)} %copy.47), calls=%async_computation | async-start | bytes 1769472 | tf_op jit(solution)/shard_map/all_to_all | solution.py:69
  38.9 1.0 copy-start
  48.2 5.3 %copy-start.1 = (bf16[2,3,96,2,384]{4,2,0,3,1:T(8,128)(2,1)S(1)}, bf16[2,3,96,2,384]{4,2,0,3,1:T(8,128)(2,1)}, u32[]{:S(2)}) copy-start(bf16[2,3,96,2,384]{4,2,0,3,1:T(8,128)(2,1)} %copy-done) | copy-start | bytes 2654212
  48.2 58.4 %all-to-all-start.1 = ((bf16[4,2,192,2,384]{4,3,2,1,0:T(2,128)(2,1)}), bf16[4,2,192,2,384]{4,3,2,1,0:T(2,128)(2,1)}, u32[]{:S(2)}, u32[]{:S(2)}) async-start(bf16[4,2,192,2,384]{4,3,2,1,0:T(2,128)(2,1)} %reshape.312), calls=%async_computation.1 | async-start | bytes 4718592 | tf_op jit(solution)/shard_map/all_to_all | solution.py:94
  53.4 2.6 %collective-permute-start = (bf16[3,192,2,384]{3,1,2,0:T(8,128)(2,1)S(1)}, bf16[3,192,2,384]{3,1,2,0:T(8,128)(2,1)}, u32[]{:S(2)}, u32[]{:S(2)}) collective-permute-start(bf16[3,192,2,384]{3,1,2,0:T(8,128)(2,1)S(1)} %bitcast.200), channel_id=1, source_target_pairs={{0,1},{1,0},{2,3},{3,2},{4,5},{5,4},{6,7},{7,6},{8,9},{9,8},{10,11... | collective-permute-start | bytes 2654216 | tf_op jit(solution)/shard_map/ppermute | solution.py:15
  57.8 52.2 %copy-start.11 = (s32[1,1,4]{2,1,0:T(1,128)S(1)}, s32[1,1,4]{2,1,0:T(1,128)}, u32[]{:S(2)}) copy-start(s32[1,1,4]{2,1,0:T(1,128)} %param.19) | copy-start | bytes 52
  110.0 29.0 %copy-start.3 = (s32[1,1,4,2]{2,3,1,0:T(2,128)S(1)}, s32[1,1,4,2]{2,3,1,0:T(2,128)}, u32[]{:S(2)}) copy-start(s32[1,1,4,2]{2,3,1,0:T(2,128)} %param.20) | copy-start | bytes 100
  138.9 2.9 %collective-permute-start.1 = (bf16[4,192,2,384]{3,1,2,0:T(8,128)(2,1)S(1)}, bf16[4,192,2,384]{3,1,2,0:T(8,128)(2,1)S(1)}, u32[]{:S(2)}, u32[]{:S(2)}) collective-permute-start(bf16[4,192,2,384]{3,1,2,0:T(8,128)(2,1)S(1)} %get-tuple-element.67), channel_id=1, source_target_pairs={{0,1},{1,0},{2,3},{3,2},{4,5},{5,4},{6,7},{7,6},{8,9},{9,8},{10,11... | collective-permute-start | bytes 3538952 | tf_op jit(solution)/shard_map/ppermute | solution.py:15
  139.6 0.8 copy-start.5
  142.3 2.3 %copy-start.4 = (pred[4]{0:T(512)(128)(4,1)S(1)}, pred[4]{0:T(512)(128)(4,1)}, u32[]{:S(2)}) copy-start(pred[4]{0:T(512)(128)(4,1)} %get-tuple-element.122) | copy-start | bytes 16
  144.6 2.0 %copy-start.7 = (f32[4,2]{1,0:T(4,128)S(1)}, f32[4,2]{1,0:T(4,128)}, u32[]{:S(2)}) copy-start(f32[4,2]{1,0:T(4,128)} %custom-call.6) | copy-start | bytes 100
  146.6 14.0 %copy-start.6 = (s32[8,4]{0,1:T(4,128)S(1)}, s32[8,4]{0,1:T(4,128)}, u32[]{:S(2)}) copy-start(s32[8,4]{0,1:T(4,128)} %param.21) | copy-start | bytes 388
where the time goes:
time: 193 us; the launch traced here: 192 us
  waiting for transfers between devices  63.7 us (33%)
  local copies, waits for them, and re-layouts  48.3 us (25%)
  blocking collectives  31.4 us (16%)
  loops' own time  16 us (8%)
  matrix products  14 us (7%)
  starting transfers between devices  9.53 us (5%)
  other arithmetic  8.41 us (4%)
    all_to_all x1, waiting for transfers between devices, shards(): lax.all_to_all(outgoing_first, 'wide', split_axis=0, concat_axis=0, tiled...  48.7 us
    psum x1, blocking collectives, shards(): diagrams = lax.psum(partial_sums, ('wide', 'col', 'pair'))  31.4 us
    another operation x1, loops' own time, shards(): level_two = lax.map(one_task, (pool_index, second_slots))  15.8 us
    all_to_all x1, waiting for transfers between devices, shards(): lax.all_to_all(outgoing, 'col', split_axis=0, concat_axis=2, tiled=True)[0]  12.3 us
    slice x1, local copies, waits for them, and re-layouts, complex_rows(): right_real = right[:, 0, :]  6.52 us
    all_to_all x1, starting transfers between devices, shards(): lax.all_to_all(outgoing_first, 'wide', split_axis=0, concat_axis=0, tiled...  5.25 us
    dynamic_slice x8, local copies, waits for them, and re-layouts, shards(): level_two = lax.map(one_task, (pool_index, second_slots))  4.7 us
    squeeze x8, local copies, waits for them, and re-layouts, shards(): products, traces = lax.map(one_product, (left_ops, right_ops))  4.24 us
  transfers between devices with their start and end apart: 4, of which 4 were waited for; matrix products, arithmetic and copies ran while one was open for 2% of the time, Pallas kernels for 0%

commit v1 on v0

v1 whole, which is shorter than its diff:
```python
import math

import jax
import jax.numpy as jnp
from jax import lax
from jax.experimental import pallas as pl
from jax.experimental.pallas import tpu as pltpu
from jax.sharding import PartitionSpec as P

CAP_LANE = 3
MESH = pl.DeviceIdType.MESH


def contract(
    lanes,
    peers,
    perams_ref,
    elems_ref,
    weights_ref,
    l1_peram,
    l1_elem,
    owners,
    first_ops,
    second_ops,
    product_ops,
    out_ref,
    diag_ref,
    big_elem,
    x_stage,
    own,
    arrived,
    paired,
    z_stage,
    pool,
    big_right,
    q_own,
    q_other,
    big_q,
    mask,
    term,
    terms,
    x_send,
    x_recv,
    p_send,
    p_recv,
    z_send,
    z_recv,
    q_send,
    q_recv,
    d_send,
    d_recv,
):
    here = lax.axis_index("wide")
    lane = lax.axis_index("col")
    half = lax.axis_index("pair")
    nelem, nvec, wide2 = elems_ref.shape
    rows = perams_ref.shape[1]
    half_rows = lanes * rows
    nblocks = owners.shape[1]
    tasks = second_ops.shape[2]
    nproducts = product_ops.shape[2]
    factor = 1.0 / math.sqrt(2.0 * nvec)
    total = peers * lanes * 2
    mine = (here * lanes + lane) * 2 + half

    def coords(index):
        return {"wide": index // (lanes * 2), "col": index // 2 % lanes, "pair": index % 2}

    barrier = pltpu.get_barrier_semaphore()

    def greet(i, carry):
        other = lax.rem(mine + 1 + i, total)
        pl.semaphore_signal(barrier, inc=1, device_id=coords(other), device_id_type=MESH)
        return carry

    lax.fori_loop(0, total - 1, greet, 0)

    def flat(block):
        if rows % 16 == 0:
            return block.reshape(-1, wide2)
        return block.astype(jnp.float32).reshape(-1, wide2).astype(jnp.bfloat16)

    def split(block):
        return block.reshape(lanes, rows, wide2)

    def expand(target, y):
        target[:nvec, :] = y
        target[nvec:, :nvec] = -y[:, nvec:]
        target[nvec:, nvec:] = y[:, :nvec]

    for e in range(nelem):
        expand(big_elem.at[e], elems_ref[e])

    def blocks_of(which):
        found = [jnp.int32(0)] * CAP_LANE
        count = jnp.int32(0)
        for b in range(nblocks):
            match = (owners[0, b] == which).astype(jnp.int32)
            for k in range(CAP_LANE):
                found[k] = jnp.where((match == 1) & (count == k), jnp.int32(b), found[k])
            count = count + match
        return found

    def level_one(b):
        left = perams_ref[l1_peram[0, b]]
        return jnp.dot(
            left, big_elem[l1_elem[0, b]], preferred_element_type=jnp.float32
        ).astype(jnp.bfloat16)

    def x_copy(j, k):
        return pltpu.make_async_remote_copy(
            src_ref=x_stage.at[j, k],
            dst_ref=arrived.at[lane, k],
            send_sem=x_send.at[j, k],
            recv_sem=x_recv.at[j, k],
            device_id={"col": lax.rem(lane + 1 + j, lanes)},
            device_id_type=MESH,
        )

    def p_copy(j):
        q = lax.rem(lane + lanes - j, lanes)
        return pltpu.make_async_remote_copy(
            src_ref=own if j == 0 else arrived.at[q],
            dst_ref=paired.at[q],
            send_sem=p_send.at[j],
            recv_sem=p_recv.at[j],
            device_id={"pair": 1 - half},
            device_id_type=MESH,
        )

    def z_copy(i, j):
        q = lax.rem(lane + lanes - j, lanes)
        return pltpu.make_async_remote_copy(
            src_ref=z_stage.at[i, q],
            dst_ref=pool.at[here, q],
            send_sem=z_send.at[i, j],
            recv_sem=z_recv.at[i, j],
            device_id={"wide": lax.rem(here + 1 + i, peers)},
            device_id_type=MESH,
        )

    def q_copy(t):
        return pltpu.make_async_remote_copy(
            src_ref=q_own.at[t],
            dst_ref=q_other.at[t],
            send_sem=q_send.at[t],
            recv_sem=q_recv.at[t],
            device_id={"pair": 1 - half},
            device_id_type=MESH,
        )

    def d_copy(i):
        return pltpu.make_async_remote_copy(
            src_ref=term,
            dst_ref=terms.at[mine],
            send_sem=d_send.at[i],
            recv_sem=d_recv.at[i],
            device_id=coords(lax.rem(mine + 1 + i, total)),
            device_id_type=MESH,
        )

    def rank_for(group):
        chosen = jnp.int32(0)
        for t in range(tasks):
            entry = first_ops[group, 0, t]
            chosen = jnp.where(entry // CAP_LANE == here, entry % CAP_LANE, chosen)
        return chosen

    ready = False
    for j in range(lanes - 1):
        picked = blocks_of(lax.rem(lane + 1 + j, lanes))
        for k in range(CAP_LANE):
            x_stage[j, k] = level_one(picked[k])
            if not ready:
                pl.semaphore_wait(barrier, total - 1)
                ready = True
            x_copy(j, k).start()
    picked = blocks_of(lane)
    for k in range(CAP_LANE):
        block = level_one(picked[k])
        own[k] = block
        arrived[lane, k] = block
    ranks = [rank_for(lax.rem(here + 1 + i, peers)) for i in range(peers - 1)]
    rank_here = rank_for(here)
    for i in range(peers - 1):
        z_stage[i, lane] = own[ranks[i]]
        z_copy(i, 0).start()
    p_copy(0).start()
    pool[here, lane] = own[rank_here]

    row_ids = lax.broadcasted_iota(jnp.int32, (rows, nvec), 0)
    col_ids = lax.broadcasted_iota(jnp.int32, (rows, nvec), 1)
    for q in range(lanes):
        mask[q * rows : (q + 1) * rows, :] = (
            col_ids == row_ids + (2 * q + half) * rows
        ).astype(jnp.float32)

    for j in range(lanes - 1):
        for k in range(CAP_LANE):
            x_copy(j, k).wait_recv()
    for j in range(1, lanes):
        q = lax.rem(lane + lanes - j, lanes)
        for i in range(peers - 1):
            z_stage[i, q] = arrived[q, ranks[i]]
            z_copy(i, j).start()
        p_copy(j).start()
        pool[here, q] = arrived[q, rank_here]
    for j in range(lanes):
        p_copy(j).wait_recv()

    lower = (half == 0).astype(jnp.float32)

    def both_halves(target, mine_half, other_half):
        pieces = []
        for q in range(lanes):
            a = mine_half(q).astype(jnp.float32)
            b = other_half(q).astype(jnp.float32)
            pieces.append(jnp.where(lower > 0.5, a, b))
            pieces.append(jnp.where(lower > 0.5, b, a))
        expand(target, jnp.concatenate(pieces, axis=0).astype(jnp.bfloat16))

    for k in range(CAP_LANE):
        both_halves(big_right.at[k], lambda q: arrived[q, k], lambda q: paired[q, k])

    for j in range(lanes):
        for i in range(peers - 1):
            z_copy(i, j).wait_recv()

    def one_task(t, carry):
        left = flat(pool[first_ops[here, 0, t] // CAP_LANE])
        full = jnp.dot(left, big_right[second_ops[0, 0, t]], preferred_element_type=jnp.float32)
        q_own[t] = split(full * factor).astype(jnp.bfloat16)
        q_copy(t).start()
        return carry

    lax.fori_loop(0, tasks, one_task, 0)

    for j in range(lanes - 1):
        for k in range(CAP_LANE):
            x_copy(j, k).wait_send()
    for j in range(lanes):
        p_copy(j).wait_send()
        for i in range(peers - 1):
            z_copy(i, j).wait_send()

    def q_done(t, carry):
        q_copy(t).wait()
        return carry

    lax.fori_loop(0, tasks, q_done, 0)
    term[...] = jnp.zeros_like(term)

    for v in range(nproducts):
        left_id = product_ops[0, 0, v, 0]
        right_id = product_ops[0, 0, v, 1]
        both_halves(big_q, lambda q: q_own[right_id, q], lambda q: q_other[right_id, q])
        full = jnp.dot(flat(q_own[left_id]), big_q[...], preferred_element_type=jnp.float32) * factor
        out_ref[v] = split(full).astype(jnp.bfloat16)
        weight = weights_ref[:, v : v + 1].astype(jnp.float32)
        for part in range(2):
            picked_diag = jnp.sum(
                full[:, part * nvec : (part + 1) * nvec] * mask[...], axis=0, keepdims=True
            )
            folded = sum(picked_diag[:, n : n + 128] for n in range(0, nvec, 128))
            term[:, part * 128 : (part + 1) * 128] += weight * folded

    terms[mine] = term[...]

    def d_start(i, carry):
        d_copy(i).start()
        return carry

    def d_done(i, carry):
        d_copy(i).wait()
        return carry

    lax.fori_loop(0, total - 1, d_start, 0)
    lax.fori_loop(0, total - 1, d_done, 0)
    summed = lax.fori_loop(0, total, lambda i, acc: acc + terms[i], jnp.zeros_like(term))
    diag_ref[:, 0:1] = jnp.sum(summed[:, :128], axis=1, keepdims=True) / nvec
    diag_ref[:, 1:2] = jnp.sum(summed[:, 128:], axis=1, keepdims=True) / nvec


def shards(peram, elements, l1_peram, l1_elem, owners, first_ops, second_ops, product_ops, weights):
    nelem, nvec = elements.shape[:2]
    nperam, rows = peram.shape[:2]
    lanes = lax.axis_size("col")
    peers = lax.axis_size("wide")
    tasks = second_ops.shape[2]
    nproducts = product_ops.shape[2]
    diagrams = weights.shape[0]
    width = 2 * nvec
    total = peers * lanes * 2
    vmem = pl.BlockSpec(memory_space=pltpu.VMEM)
    smem = pl.BlockSpec(memory_space=pltpu.SMEM)
    bf16 = jnp.bfloat16

    def kernel(*refs):
        contract(lanes, peers, *refs)

    products, sums = pl.pallas_call(
        kernel,
        out_shape=(
            jax.ShapeDtypeStruct((nproducts, lanes, rows, width), bf16),
            jax.ShapeDtypeStruct((diagrams, 2), jnp.float32),
        ),
        in_specs=[vmem] * 3 + [smem] * 6,
        out_specs=(vmem, vmem),
        scratch_shapes=[
            pltpu.VMEM((nelem, width, width), bf16),
            pltpu.VMEM((max(lanes - 1, 1), CAP_LANE, rows, width), bf16),
            pltpu.VMEM((CAP_LANE, rows, width), bf16),
            pltpu.VMEM((lanes, CAP_LANE, rows, width), bf16),
            pltpu.VMEM((lanes, CAP_LANE, rows, width), bf16),
            pltpu.VMEM((peers, lanes, rows, width), bf16),
            pltpu.VMEM((peers, lanes, rows, width), bf16),
            pltpu.VMEM((CAP_LANE, width, width), bf16),
            pltpu.VMEM((tasks, lanes, rows, width), bf16),
            pltpu.VMEM((tasks, lanes, rows, width), bf16),
            pltpu.VMEM((width, width), bf16),
            pltpu.VMEM((lanes * rows, nvec), jnp.float32),
            pltpu.VMEM((diagrams, 256), jnp.float32),
            pltpu.VMEM((total, diagrams, 256), jnp.float32),
            pltpu.SemaphoreType.DMA((lanes, CAP_LANE)),
            pltpu.SemaphoreType.DMA((lanes, CAP_LANE)),
            pltpu.SemaphoreType.DMA((lanes,)),
            pltpu.SemaphoreType.DMA((lanes,)),
            pltpu.SemaphoreType.DMA((peers, lanes)),
            pltpu.SemaphoreType.DMA((peers, lanes)),
            pltpu.SemaphoreType.DMA((tasks,)),
            pltpu.SemaphoreType.DMA((tasks,)),
            pltpu.SemaphoreType.DMA((total,)),
            pltpu.SemaphoreType.DMA((total,)),
        ],
        compiler_params=pltpu.CompilerParams(
            collective_id=0, has_side_effects=True, vmem_limit_bytes=58 * 2**20
        ),
    )(
        peram.reshape(nperam, rows, width),
        elements.reshape(nelem, nvec, width),
        weights,
        l1_peram,
        l1_elem,
        owners,
        first_ops,
        second_ops,
        product_ops,
    )
    return (products.reshape(nproducts, lanes, 1, rows, 2, nvec), sums)


def solution(mesh):
    placed = (
        P(("parts", "wide"), ("col", "pair"), None, None),
        P("parts", None, None, None),
        P(("parts", "wide"), None),
        P(("parts", "wide"), None),
        P(("parts", "wide"), None),
        P("parts", "col", None),
        P(("parts", "wide"), "col", None),
        P(("parts", "wide"), "col", None, None),
        P("parts", ("wide", "col")),
    )
    return jax.shard_map(
        shards,
        mesh=mesh,
        in_specs=placed,
        out_specs=(P(("parts", "wide", "col"), None, "pair", None, None, None), P("parts", None)),
        check_vma=False,
    )
```

time: 193 us -> 63.8 us (0.33)
  waiting for transfers between devices: 63.7 us -> 0 us
  Pallas kernels: 0 us -> 46.7 us
  local copies, waits for them, and re-layouts: 48.3 us -> 16.1 us
  blocking collectives: 31.4 us -> 0 us
  loops' own time: 16 us -> 0 us
  matrix products: 14 us -> 0 us
  starting transfers between devices: 9.53 us -> 0 us
  other arithmetic: 8.41 us -> 0 us
    all_to_all x2 -> x0, waiting for transfers between devices: 61 us -> none  [the longest x1 48.7 us: shards(): lax.all_to_all(outgoing_first, 'wide', split_axis=0, concat_axis=0, tiled...]
    pallas_call x0 -> x1, Pallas kernels: none -> 46.7 us  [shards(): pl.pallas_call(kernel, out_shape=(jax.ShapeDtypeStruct((nproducts, lanes,...]
    psum x1 -> x0, blocking collectives: 31.4 us -> none  [shards(): diagrams = lax.psum(partial_sums, ('wide', 'col', 'pair'))]
    another operation x2 -> x0, loops' own time: 16 us -> none  [the longest x1 15.8 us: shards(): level_two = lax.map(one_task, (pool_index, second_slots))]
    dot_general x39 -> x0, matrix products: 14 us -> none  [the longest x9 2.7 us: complex_rows(): jnp.dot(left_imag, right_real, preferred_element_type=jnp.float32)]
    all_to_all x2 -> x0, starting transfers between devices: 9.45 us -> none  [the longest x1 5.25 us: shards(): lax.all_to_all(outgoing_first, 'wide', split_axis=0, concat_axis=0, tiled...]
    squeeze x16 -> x0, local copies, waits for them, and re-layouts: 8.49 us -> none  [the longest x8 4.24 us: shards(): products, traces = lax.map(one_product, (left_ops, right_ops))]
    slice x1 -> x0, local copies, waits for them, and re-layouts: 6.52 us -> none  [complex_rows(): right_real = right[:, 0, :]]
  transfers between devices with their start and end apart: 4 -> 0, of which waited for: 4 -> 0; matrix products, arithmetic and copies ran while one was open for 2% -> 0% of each run, Pallas kernels for 0% -> 0%
where the time goes in v1:
time: 63.8 us; the launch traced here: 63.5 us
  Pallas kernels  46.7 us (73%)
  local copies, waits for them, and re-layouts  16.1 us (25%)
  between operations  0.65 us (1%)
    pallas_call x1, Pallas kernels, shards(): pl.pallas_call(kernel, out_shape=(jax.ShapeDtypeStruct((nproducts, lanes,...  46.7 us
    reshape x1, local copies, waits for them, and re-layouts, shards(): elements.reshape(nelem, nvec, width)  6.43 us
    reshape x1, local copies, waits for them, and re-layouts, shards(): return (products.reshape(nproducts, lanes, 1, rows, 2, nvec), sums)  3.57 us
    unnamed x5, local copies, waits for them, and re-layouts  3.31 us
    reshape x1, local copies, waits for them, and re-layouts, shards(): peram.reshape(nperam, rows, width)  2.76 us

profile of v1, /device:TPU:0, one launch (start us, length us, event | category | flops | bytes accessed | tf_op | source)
XLA Modules:
  0.0 63.5 jit_solution(13446749123913964875)
XLA Ops:
  0.6 1.3 %copy.12.refs_8_ = s32[1,1,4,2]{3,2,1,0:T(4,128)} copy(s32[1,1,4,2]{2,3,1,0:T(2,128)} %param.16) | data formatting | bytes 64 | tf_op args[7]
  2.0 1.3 %copy.11.refs_2_ = s32[8,4]{1,0:T(8,128)} copy(s32[8,4]{0,1:T(4,128)} %param.17) | data formatting | bytes 256 | tf_op args[8]
  3.3 2.8 %reshape.13.refs_0_ = bf16[4,96,768]{2,1,0:T(8,128)(2,1)} reshape(bf16[4,96,2,384]{3,2,1,0:T(2,128)(2,1)} %param.9) | data formatting | bytes 1179648 | tf_op jit(solution)/shard_map/reshape | solution.py:339
  6.1 6.4 %reshape.14.refs_1_ = bf16[4,384,768]{2,1,0:T(8,128)(2,1)} reshape(bf16[4,384,2,384]{3,2,1,0:T(2,128)(2,1)} %param.10) | data formatting | bytes 4718592 | tf_op jit(solution)/shard_map/reshape | solution.py:340
  12.5 46.7 %shard_map.104 = (bf16[4,2,96,768]{3,2,1,0:T(8,128)(2,1)}, f32[8,2]{1,0:T(8,128)}) custom-call(bf16[4,96,768]{2,1,0:T(8,128)(2,1)} %reshape.13.refs_0_, bf16[4,384,768]{2,1,0:T(8,128)(2,1)} %reshape.14.refs_1_, s32[8,4]{1,0:T(8,128)} %copy.11.refs_2_, s32[1,4]{1,0:T(1,128)} %refs_3_.1, s32[1,4]{1,0:T(1,128)} %refs_4_.1, s32[1,4]{1,0:T(1,128)} %refs_5_.1, ...), custom_call_target="tpu_custom_call" | custom-call | tf_op jit(solution)/shard_map/pallas_call | solution.py:301
  59.2 0.0 copy-start
  59.2 3.6 %reshape.15 = bf16[4,2,1,96,2,384]{5,4,3,1,0,2:T(2,128)(2,1)} reshape(bf16[4,2,96,768]{3,2,1,0:T(8,128)(2,1)} %get-tuple-element.4) | data formatting | bytes 2359296 | tf_op jit(solution)/shard_map/reshape | solution.py:349
  62.8 0.0 copy-done
  62.8 0.6 %copy.14 = f32[8,2]{0,1:T(2,128)} copy(f32[8,2]{1,0:T(8,128)S(1)} %copy-done) | data formatting | bytes 128
Async XLA Ops:
  59.2 3.6 %copy-start = (f32[8,2]{1,0:T(8,128)S(1)}, f32[8,2]{1,0:T(8,128)}, u32[]{:S(2)}) copy-start(f32[8,2]{1,0:T(8,128)} %get-tuple-element.7) | copy-start | bytes 196

commit v2 on v1

--- a/solution.py
+++ b/solution.py
@@ -17,6 +17,8 @@
     perams_ref,
     elems_ref,
     weights_ref,
+    l1_elem_vec,
+    owners_vec,
     l1_peram,
     l1_elem,
     owners,
@@ -25,6 +27,7 @@
     product_ops,
     out_ref,
     diag_ref,
+    elems_raw,
     big_elem,
     x_stage,
     own,
@@ -32,6 +35,11 @@
     paired,
     z_stage,
     pool,
+    half_raw,
+    full_raw,
+    left_wide,
+    right_wide,
+    left_ops,
     big_right,
     q_own,
     q_other,
@@ -39,12 +47,18 @@
     mask,
     term,
     terms,
+    ids_vec,
+    ids,
+    e_sem,
+    ids_sem,
     x_send,
     x_recv,
     p_send,
     p_recv,
     z_send,
     z_recv,
+    i_send,
+    i_recv,
     q_send,
     q_recv,
     d_send,
@@ -53,15 +67,25 @@
     here = lax.axis_index("wide")
     lane = lax.axis_index("col")
     half = lax.axis_index("pair")
-    nelem, nvec, wide2 = elems_ref.shape
+    nelem = elems_ref.shape[0]
+    nvec = left_wide.shape[1] // 2
+    wide2 = 2 * nvec
     rows = perams_ref.shape[1]
+    strips = nvec // 128
     half_rows = lanes * rows
     nblocks = owners.shape[1]
     tasks = second_ops.shape[2]
-    nproducts = product_ops.shape[2]
+    nproducts = product_ops.shape[3]
     factor = 1.0 / math.sqrt(2.0 * nvec)
     total = peers * lanes * 2
     mine = (here * lanes + lane) * 2 + half
+    bf16 = jnp.bfloat16
+
+    def elem_copy(e):
+        return pltpu.make_async_copy(elems_ref.at[e], elems_raw.at[e], e_sem.at[e])
+
+    for e in range(nelem):
+        elem_copy(e).start()
 
     def coords(index):
         return {"wide": index // (lanes * 2), "col": index // 2 % lanes, "pair": index % 2}
@@ -78,7 +102,7 @@
     def flat(block):
         if rows % 16 == 0:
             return block.reshape(-1, wide2)
-        return block.astype(jnp.float32).reshape(-1, wide2).astype(jnp.bfloat16)
+        return block.astype(jnp.float32).reshape(-1, wide2).astype(bf16)
 
     def split(block):
         return block.reshape(lanes, rows, wide2)
@@ -88,24 +112,30 @@
         target[nvec:, :nvec] = -y[:, nvec:]
         target[nvec:, nvec:] = y[:, :nvec]
 
-    for e in range(nelem):
-        expand(big_elem.at[e], elems_ref[e])
-
-    def blocks_of(which):
+    def strip(j, base=0):
+        return slice(base + j * 128, base + (j + 1) * 128)
+
+    def columns(raw, count):
+        for j in range(strips):
+            for c in range(2):
+                yield c, j, raw[j, pl.ds(c, count, stride=2), :].astype(bf16)
+
+    def gather_columns(target, raw):
+        for c, j, block in columns(raw, target.shape[0]):
+            target[:, strip(j, c * nvec)] = block
+
+    def as_rows(block):
+        return block.astype(jnp.float32).reshape(-1, 128)
+
+    def blocks_of(which, owner_at):
         found = [jnp.int32(0)] * CAP_LANE
         count = jnp.int32(0)
         for b in range(nblocks):
-            match = (owners[0, b] == which).astype(jnp.int32)
+            match = (owner_at(b) == which).astype(jnp.int32)
             for k in range(CAP_LANE):
                 found[k] = jnp.where((match == 1) & (count == k), jnp.int32(b), found[k])
             count = count + match
         return found
-
-    def level_one(b):
-        left = perams_ref[l1_peram[0, b]]
-        return jnp.dot(
-            left, big_elem[l1_elem[0, b]], preferred_element_type=jnp.float32
-        ).astype(jnp.bfloat16)
 
     def x_copy(j, k):
         return pltpu.make_async_remote_copy(
@@ -139,6 +169,16 @@
             device_id_type=MESH,
         )
 
+    def i_copy(i):
+        return pltpu.make_async_remote_copy(
+            src_ref=ids_vec.at[here],
+            dst_ref=ids_vec.at[here],
+            send_sem=i_send.at[i],
+            recv_sem=i_recv.at[i],
+            device_id={"wide": lax.rem(here + 1 + i, peers)},
+            device_id_type=MESH,
+        )
+
     def q_copy(t):
         return pltpu.make_async_remote_copy(
             src_ref=q_own.at[t],
@@ -166,20 +206,24 @@
             chosen = jnp.where(entry // CAP_LANE == here, entry % CAP_LANE, chosen)
         return chosen
 
+    ids_vec[here] = jnp.zeros(ids_vec.shape[1:], jnp.int32)
+    ids_vec[here, 0:1, 0:nblocks] = l1_elem_vec[...]
+    ids_vec[here, 1:2, 0:nblocks] = owners_vec[...]
     ready = False
     for j in range(lanes - 1):
-        picked = blocks_of(lax.rem(lane + 1 + j, lanes))
+        picked = blocks_of(lax.rem(lane + 1 + j, lanes), lambda b: owners[0, b])
         for k in range(CAP_LANE):
-            x_stage[j, k] = level_one(picked[k])
+            x_stage[j, k] = perams_ref[l1_peram[0, picked[k]]]
             if not ready:
                 pl.semaphore_wait(barrier, total - 1)
                 ready = True
             x_copy(j, k).start()
-    picked = blocks_of(lane)
+    for i in range(peers - 1):
+        i_copy(i).start()
+    picked = blocks_of(lane, lambda b: owners[0, b])
     for k in range(CAP_LANE):
-        block = level_one(picked[k])
+        block = perams_ref[l1_peram[0, picked[k]]]
         own[k] = block
-        arrived[lane, k] = block
     ranks = [rank_for(lax.rem(here + 1 + i, peers)) for i in range(peers - 1)]
     rank_here = rank_for(here)
     for i in range(peers - 1):
@@ -195,6 +239,20 @@
             col_ids == row_ids + (2 * q + half) * rows
         ).astype(jnp.float32)
 
+    def convert_elem(e):
+        elem_copy(e).wait()
+        for j in range(strips):
+            full_raw[j] = as_rows(elems_raw[e, :, :, strip(j)])
+        for c, j, block in columns(full_raw, nvec):
+            low, high = j * 128, (j + 1) * 128
+            if c == 0:
+                big_elem[e, :nvec, low:high] = block
+                big_elem[e, nvec:, nvec + low : nvec + high] = block
+            else:
+                big_elem[e, :nvec, nvec + low : nvec + high] = block
+                big_elem[e, nvec:, low:high] = -block
+
+    convert_elem(0)
     for j in range(lanes - 1):
         for k in range(CAP_LANE):
             x_copy(j, k).wait_recv()
@@ -205,31 +263,73 @@
             z_copy(i, j).start()
         p_copy(j).start()
         pool[here, q] = arrived[q, rank_here]
+    for e in range(1, nelem):
+        convert_elem(e)
+    for i in range(peers - 1):
+        i_copy(i).wait()
+    ids_copy = pltpu.make_async_copy(ids_vec, ids, ids_sem)
+    ids_copy.start()
+    ids_copy.wait()
     for j in range(lanes):
         p_copy(j).wait_recv()
 
-    lower = (half == 0).astype(jnp.float32)
-
-    def both_halves(target, mine_half, other_half):
-        pieces = []
-        for q in range(lanes):
-            a = mine_half(q).astype(jnp.float32)
-            b = other_half(q).astype(jnp.float32)
-            pieces.append(jnp.where(lower > 0.5, a, b))
-            pieces.append(jnp.where(lower > 0.5, b, a))
-        expand(target, jnp.concatenate(pieces, axis=0).astype(jnp.bfloat16))
-
     for k in range(CAP_LANE):
-        both_halves(big_right.at[k], lambda q: arrived[q, k], lambda q: paired[q, k])
-
-    for j in range(lanes):
-        for i in range(peers - 1):
+        for n in range(lanes):
+            q = lax.rem(lane + lanes - n, lanes)
+            for side in range(2):
+                at = half if side == 0 else 1 - half
+                start = pl.multiple_of((2 * q + at) * (2 * rows), 8)
+                for j in range(strips):
+                    if side == 1:
+                        block = paired[q, k, :, :, strip(j)]
+                    elif n == 0:
+                        block = own[k, :, :, strip(j)]
+                    else:
+                        block = arrived[q, k, :, :, strip(j)]
+                    full_raw[j, pl.ds(start, 2 * rows), :] = as_rows(block)
+        gather_columns(right_wide, full_raw)
+        block = jnp.dot(
+            right_wide[...],
+            big_elem[l1_elem[0, picked[k]]],
+            preferred_element_type=jnp.float32,
+        )
+        expand(big_right.at[k], block.astype(bf16))
+
+    def source_element(source):
+        wanted = jnp.int32(0)
+        for t in range(tasks):
+            entry = first_ops[here, 0, t]
+            wanted = jnp.where(entry // CAP_LANE == source, entry % CAP_LANE, wanted)
+        found = blocks_of(lane, lambda b: ids[source, 1, b])
+        chosen = found[0]
+        for k in range(1, CAP_LANE):
+            chosen = jnp.where(wanted == k, found[k], chosen)
+        return ids[source, 0, chosen]
+
+    def make_left(source):
+        for j in range(strips):
+            half_raw[j] = as_rows(pool[source, :, :, :, strip(j)])
+        gather_columns(left_wide, half_raw)
+        left_ops[source] = jnp.dot(
+            left_wide[...],
+            big_elem[source_element(source)],
+            preferred_element_type=jnp.float32,
+        ).astype(bf16)
+
+    make_left(here)
+
+    def one_source(i, carry):
+        for j in range(lanes):
             z_copy(i, j).wait_recv()
+        make_left(lax.rem(here + peers - 1 - i, peers))
+        return carry
+
+    lax.fori_loop(0, peers - 1, one_source, 0)
 
     def one_task(t, carry):
-        left = flat(pool[first_ops[here, 0, t] // CAP_LANE])
+        left = left_ops[first_ops[here, 0, t] // CAP_LANE]
         full = jnp.dot(left, big_right[second_ops[0, 0, t]], preferred_element_type=jnp.float32)
-        q_own[t] = split(full * factor).astype(jnp.bfloat16)
+        q_own[t] = split(full * factor).astype(bf16)
         q_copy(t).start()
         return carry
 
@@ -248,22 +348,37 @@
         return carry
 
     lax.fori_loop(0, tasks, q_done, 0)
-    term[...] = jnp.zeros_like(term)
-
+
+    def both_halves(target, mine_half, other_half):
+        pieces = []
+        for q in range(lanes):
+            a = mine_half(q).astype(jnp.float32)
+            b = other_half(q).astype(jnp.float32)
+            pieces.append(jnp.where(half == 0, a, b))
+            pieces.append(jnp.where(half == 0, b, a))
+        expand(target, jnp.concatenate(pieces, axis=0).astype(bf16))
+
+    sums = [jnp.zeros((1, term.shape[1]), jnp.float32)] * 2
     for v in range(nproducts):
-        left_id = product_ops[0, 0, v, 0]
-        right_id = product_ops[0, 0, v, 1]
+        left_id = product_ops[0, 0, 0, v]
+        right_id = product_ops[0, 0, 1, v]
         both_halves(big_q, lambda q: q_own[right_id, q], lambda q: q_other[right_id, q])
         full = jnp.dot(flat(q_own[left_id]), big_q[...], preferred_element_type=jnp.float32) * factor
-        out_ref[v] = split(full).astype(jnp.bfloat16)
-        weight = weights_ref[:, v : v + 1].astype(jnp.float32)
-        for part in range(2):
+        weight = weights_ref[v : v + 1, :].astype(jnp.float32)
+        for c in range(2):
+            for j in range(strips):
+                half_raw[j, pl.ds(c, half_rows, stride=2), :] = full[:, strip(j, c * nvec)]
             picked_diag = jnp.sum(
-                full[:, part * nvec : (part + 1) * nvec] * mask[...], axis=0, keepdims=True
+                full[:, c * nvec : (c + 1) * nvec] * mask[...], axis=0, keepdims=True
             )
-            folded = sum(picked_diag[:, n : n + 128] for n in range(0, nvec, 128))
-            term[:, part * 128 : (part + 1) * 128] += weight * folded
-
+            sums[c] = sums[c] + weight * jnp.sum(picked_diag, axis=1, keepdims=True)
+        for j in range(strips):
+            out_ref[v, :, 0, :, :, strip(j)] = (
+                half_raw[j].astype(bf16).reshape(lanes, rows, 2, 128)
+            )
+
+    for c in range(2):
+        term[c : c + 1, :] = sums[c]
     terms[mine] = term[...]
 
     def d_start(i, carry):
@@ -277,8 +392,7 @@
     lax.fori_loop(0, total - 1, d_start, 0)
     lax.fori_loop(0, total - 1, d_done, 0)
     summed = lax.fori_loop(0, total, lambda i, acc: acc + terms[i], jnp.zeros_like(term))
-    diag_ref[:, 0:1] = jnp.sum(summed[:, :128], axis=1, keepdims=True) / nvec
-    diag_ref[:, 1:2] = jnp.sum(summed[:, 128:], axis=1, keepdims=True) / nvec
+    diag_ref[...] = summed / nvec
 
 
 def shards(peram, elements, l1_peram, l1_elem, owners, first_ops, second_ops, product_ops, weights):
@@ -290,10 +404,12 @@
     nproducts = product_ops.shape[2]
     diagrams = weights.shape[0]
     width = 2 * nvec
+    strips = nvec // 128
     total = peers * lanes * 2
     vmem = pl.BlockSpec(memory_space=pltpu.VMEM)
     smem = pl.BlockSpec(memory_space=pltpu.SMEM)
     bf16 = jnp.bfloat16
+    f32 = jnp.float32
 
     def kernel(*refs):
         contract(lanes, peers, *refs)
@@ -301,32 +417,44 @@
     products, sums = pl.pallas_call(
         kernel,
         out_shape=(
-            jax.ShapeDtypeStruct((nproducts, lanes, rows, width), bf16),
-            jax.ShapeDtypeStruct((diagrams, 2), jnp.float32),
+            jax.ShapeDtypeStruct((nproducts, lanes, 1, rows, 2, nvec), bf16),
+            jax.ShapeDtypeStruct((2, diagrams), f32),
         ),
-        in_specs=[vmem] * 3 + [smem] * 6,
+        in_specs=[vmem, pl.BlockSpec(memory_space=pl.ANY), vmem, vmem, vmem] + [smem] * 6,
         out_specs=(vmem, vmem),
         scratch_shapes=[
+            pltpu.VMEM((nelem, nvec, 2, nvec), bf16),
             pltpu.VMEM((nelem, width, width), bf16),
-            pltpu.VMEM((max(lanes - 1, 1), CAP_LANE, rows, width), bf16),
-            pltpu.VMEM((CAP_LANE, rows, width), bf16),
-            pltpu.VMEM((lanes, CAP_LANE, rows, width), bf16),
-            pltpu.VMEM((lanes, CAP_LANE, rows, width), bf16),
-            pltpu.VMEM((peers, lanes, rows, width), bf16),
-            pltpu.VMEM((peers, lanes, rows, width), bf16),
+            pltpu.VMEM((max(lanes - 1, 1), CAP_LANE, rows, 2, nvec), bf16),
+            pltpu.VMEM((CAP_LANE, rows, 2, nvec), bf16),
+            pltpu.VMEM((lanes, CAP_LANE, rows, 2, nvec), bf16),
+            pltpu.VMEM((lanes, CAP_LANE, rows, 2, nvec), bf16),
+            pltpu.VMEM((peers, lanes, rows, 2, nvec), bf16),
+            pltpu.VMEM((peers, lanes, rows, 2, nvec), bf16),
+            pltpu.VMEM((strips, 2 * lanes * rows, 128), f32),
+            pltpu.VMEM((strips, 2 * nvec, 128), f32),
+            pltpu.VMEM((lanes * rows, width), bf16),
+            pltpu.VMEM((nvec, width), bf16),
+            pltpu.VMEM((peers, lanes * rows, width), bf16),
             pltpu.VMEM((CAP_LANE, width, width), bf16),
             pltpu.VMEM((tasks, lanes, rows, width), bf16),
             pltpu.VMEM((tasks, lanes, rows, width), bf16),
             pltpu.VMEM((width, width), bf16),
-            pltpu.VMEM((lanes * rows, nvec), jnp.float32),
-            pltpu.VMEM((diagrams, 256), jnp.float32),
-            pltpu.VMEM((total, diagrams, 256), jnp.float32),
+            pltpu.VMEM((lanes * rows, nvec), f32),
+            pltpu.VMEM((2, diagrams), f32),
+            pltpu.VMEM((total, 2, diagrams), f32),
+            pltpu.VMEM((peers, 8, 128), jnp.int32),
+            pltpu.SMEM((peers, 8, 128), jnp.int32),
+            pltpu.SemaphoreType.DMA((nelem,)),
+            pltpu.SemaphoreType.DMA,
             pltpu.SemaphoreType.DMA((lanes, CAP_LANE)),
             pltpu.SemaphoreType.DMA((lanes, CAP_LANE)),
             pltpu.SemaphoreType.DMA((lanes,)),
             pltpu.SemaphoreType.DMA((lanes,)),
             pltpu.SemaphoreType.DMA((peers, lanes)),
             pltpu.SemaphoreType.DMA((peers, lanes)),
+            pltpu.SemaphoreType.DMA((peers,)),
+            pltpu.SemaphoreType.DMA((peers,)),
             pltpu.SemaphoreType.DMA((tasks,)),
             pltpu.SemaphoreType.DMA((tasks,)),
             pltpu.SemaphoreType.DMA((total,)),
@@ -336,17 +464,19 @@
             collective_id=0, has_side_effects=True, vmem_limit_bytes=58 * 2**20
         ),
     )(
-        peram.reshape(nperam, rows, width),
-        elements.reshape(nelem, nvec, width),
-        weights,
+        peram,
+        elements,
+        weights.T,
+        l1_elem,
+        owners,
         l1_peram,
         l1_elem,
         owners,
         first_ops,
         second_ops,
-        product_ops,
+        product_ops.transpose(0, 1, 3, 2),
     )
-    return (products.reshape(nproducts, lanes, 1, rows, 2, nvec), sums)
+    return (products, sums.T)
 
 
 def solution(mesh):

time: 63.8 us -> 51.5 us (0.81)
  local copies, waits for them, and re-layouts: 16.1 us -> 3.66 us
    reshape x3 -> x0, local copies, waits for them, and re-layouts: 12.8 us -> none  [the longest x1 6.43 us: shards(): elements.reshape(nelem, nvec, width)]
    unnamed x5 -> x4, local copies, waits for them, and re-layouts: 3.31 us -> 3.66 us
where the time goes in v2:
time: 51.5 us; the launch traced here: 51.4 us
  Pallas kernels  47.1 us (91%)
  local copies, waits for them, and re-layouts  3.66 us (7%)
  between operations  0.65 us (1%)
    pallas_call x1, Pallas kernels, shards(): pl.pallas_call(kernel, out_shape=(jax.ShapeDtypeStruct((nproducts, lanes,...  47.1 us
    unnamed x4, local copies, waits for them, and re-layouts  3.66 us

profile of v2, /device:TPU:0, one launch (start us, length us, event | category | flops | bytes accessed | tf_op | source)
XLA Modules:
  0.0 51.4 jit_solution(11404189604534641973)
XLA Ops:
  0.6 47.1 %shard_map.104 = (bf16[4,2,1,96,2,384]{5,4,3,2,1,0:T(2,128)(2,1)}, f32[2,8]{1,0:T(2,128)}) custom-call(bf16[4,96,2,384]{3,2,1,0:T(2,128)(2,1)} %refs_0_.1, bf16[4,384,2,384]{3,2,1,0:T(2,128)(2,1)} %refs_1_.1, s32[4,8]{1,0:T(4,128)} %bitcast.3, s32[1,4]{1,0:T(1,128)} %refs_6_.1, s32[1,4]{1,0:T(1,128)} %refs_7_.1, s32[1,4]{1,0:T(1,128)} %refs_5_.1, ...), custom_call_target="tpu_custom_call" | custom-call | tf_op jit(solution)/shard_map/pallas_call | solution.py:417
  47.7 0.0 copy-start
  47.7 3.1 %copy.13 = bf16[4,2,1,96,2,384]{5,4,3,2,1,0:T(2,128)(2,1)} copy(bf16[4,2,1,96,2,384]{5,4,3,2,1,0:T(2,128)(2,1)} %get-tuple-element.8) | data formatting | bytes 2359296
  50.8 0.0 copy-done
  50.8 0.6 %copy.14 = f32[8,2]{0,1:T(2,128)} copy(f32[8,2]{0,1:T(2,128)S(1)} %bitcast.5) | data formatting | bytes 128
Async XLA Ops:
  47.7 3.1 %copy-start = (f32[2,8]{1,0:T(2,128)S(1)}, f32[2,8]{1,0:T(2,128)}, u32[]{:S(2)}) copy-start(f32[2,8]{1,0:T(2,128)} %get-tuple-element.5) | copy-start | bytes 196

commit v3 on v2

--- a/solution.py
+++ b/solution.py
@@ -27,6 +27,7 @@
     product_ops,
     out_ref,
     diag_ref,
+    perams_raw,
     elems_raw,
     big_elem,
     x_stage,
@@ -49,6 +50,10 @@
     terms,
     ids_vec,
     ids,
+    r_full,
+    out_stage,
+    o_sem,
+    pe_sem,
     e_sem,
     ids_sem,
     x_send,
@@ -84,8 +89,11 @@
     def elem_copy(e):
         return pltpu.make_async_copy(elems_ref.at[e], elems_raw.at[e], e_sem.at[e])
 
-    for e in range(nelem):
-        elem_copy(e).start()
+    def out_copy(v):
+        return pltpu.make_async_copy(out_stage.at[v], out_ref.at[v], o_sem.at[v])
+
+    perams_copy = pltpu.make_async_copy(perams_ref, perams_raw, pe_sem)
+    perams_copy.start()
 
     def coords(index):
         return {"wide": index // (lanes * 2), "col": index // 2 % lanes, "pair": index % 2}
@@ -98,6 +106,8 @@
         return carry
 
     lax.fori_loop(0, total - 1, greet, 0)
+    for e in range(nelem):
+        elem_copy(e).start()
 
     def flat(block):
         if rows % 16 == 0:
@@ -209,26 +219,23 @@
     ids_vec[here] = jnp.zeros(ids_vec.shape[1:], jnp.int32)
     ids_vec[here, 0:1, 0:nblocks] = l1_elem_vec[...]
     ids_vec[here, 1:2, 0:nblocks] = owners_vec[...]
-    ready = False
+    picked = blocks_of(lane, lambda b: owners[0, b])
+    ranks = [rank_for(lax.rem(here + 1 + i, peers)) for i in range(peers - 1)]
+    rank_here = rank_for(here)
+    perams_copy.wait()
+    for k in range(CAP_LANE):
+        own[k] = perams_raw[l1_peram[0, picked[k]]]
+    pl.semaphore_wait(barrier, total - 1)
+    for i in range(peers - 1):
+        z_stage[i, lane] = own[ranks[i]]
+        z_copy(i, 0).start()
     for j in range(lanes - 1):
-        picked = blocks_of(lax.rem(lane + 1 + j, lanes), lambda b: owners[0, b])
+        others = blocks_of(lax.rem(lane + 1 + j, lanes), lambda b: owners[0, b])
         for k in range(CAP_LANE):
-            x_stage[j, k] = perams_ref[l1_peram[0, picked[k]]]
-            if not ready:
-                pl.semaphore_wait(barrier, total - 1)
-                ready = True
+            x_stage[j, k] = perams_raw[l1_peram[0, others[k]]]
             x_copy(j, k).start()
     for i in range(peers - 1):
         i_copy(i).start()
-    picked = blocks_of(lane, lambda b: owners[0, b])
-    for k in range(CAP_LANE):
-        block = perams_ref[l1_peram[0, picked[k]]]
-        own[k] = block
-    ranks = [rank_for(lax.rem(here + 1 + i, peers)) for i in range(peers - 1)]
-    rank_here = rank_for(here)
-    for i in range(peers - 1):
-        z_stage[i, lane] = own[ranks[i]]
-        z_copy(i, 0).start()
     p_copy(0).start()
     pool[here, lane] = own[rank_here]
 
@@ -365,17 +372,12 @@
         both_halves(big_q, lambda q: q_own[right_id, q], lambda q: q_other[right_id, q])
         full = jnp.dot(flat(q_own[left_id]), big_q[...], preferred_element_type=jnp.float32) * factor
         weight = weights_ref[v : v + 1, :].astype(jnp.float32)
+        r_full[v] = full
         for c in range(2):
-            for j in range(strips):
-                half_raw[j, pl.ds(c, half_rows, stride=2), :] = full[:, strip(j, c * nvec)]
             picked_diag = jnp.sum(
                 full[:, c * nvec : (c + 1) * nvec] * mask[...], axis=0, keepdims=True
             )
             sums[c] = sums[c] + weight * jnp.sum(picked_diag, axis=1, keepdims=True)
-        for j in range(strips):
-            out_ref[v, :, 0, :, :, strip(j)] = (
-                half_raw[j].astype(bf16).reshape(lanes, rows, 2, 128)
-            )
 
     for c in range(2):
         term[c : c + 1, :] = sums[c]
@@ -390,9 +392,30 @@
         return carry
 
     lax.fori_loop(0, total - 1, d_start, 0)
+    for v in range(nproducts):
+        for j in range(strips):
+            for c in range(2):
+                half_raw[j, pl.ds(c, half_rows, stride=2), :] = r_full[v, :, strip(j, c * nvec)]
+            out_stage[v, :, 0, :, :, strip(j)] = (
+                half_raw[j].astype(bf16).reshape(lanes, rows, 2, 128)
+            )
+        out_copy(v).start()
     lax.fori_loop(0, total - 1, d_done, 0)
     summed = lax.fori_loop(0, total, lambda i, acc: acc + terms[i], jnp.zeros_like(term))
     diag_ref[...] = summed / nvec
+    for v in range(nproducts):
+        out_copy(v).wait()
+
+
+def relay(source, target, sems):
+    copies = [
+        pltpu.make_async_copy(source.at[v], target.at[v], sems.at[v])
+        for v in range(source.shape[0])
+    ]
+    for copy in copies:
+        copy.start()
+    for copy in copies:
+        copy.wait()
 
 
 def shards(peram, elements, l1_peram, l1_elem, owners, first_ops, second_ops, product_ops, weights):
@@ -408,6 +431,7 @@
     total = peers * lanes * 2
     vmem = pl.BlockSpec(memory_space=pltpu.VMEM)
     smem = pl.BlockSpec(memory_space=pltpu.SMEM)
+    anywhere = pl.BlockSpec(memory_space=pl.ANY)
     bf16 = jnp.bfloat16
     f32 = jnp.float32
 
@@ -420,9 +444,10 @@
             jax.ShapeDtypeStruct((nproducts, lanes, 1, rows, 2, nvec), bf16),
             jax.ShapeDtypeStruct((2, diagrams), f32),
         ),
-        in_specs=[vmem, pl.BlockSpec(memory_space=pl.ANY), vmem, vmem, vmem] + [smem] * 6,
-        out_specs=(vmem, vmem),
+        in_specs=[anywhere] * 2 + [vmem] * 3 + [smem] * 6,
+        out_specs=(anywhere, vmem),
         scratch_shapes=[
+            pltpu.VMEM((nperam, rows, 2, nvec), bf16),
             pltpu.VMEM((nelem, nvec, 2, nvec), bf16),
             pltpu.VMEM((nelem, width, width), bf16),
             pltpu.VMEM((max(lanes - 1, 1), CAP_LANE, rows, 2, nvec), bf16),
@@ -445,6 +470,10 @@
             pltpu.VMEM((total, 2, diagrams), f32),
             pltpu.VMEM((peers, 8, 128), jnp.int32),
             pltpu.SMEM((peers, 8, 128), jnp.int32),
+            pltpu.VMEM((nproducts, lanes * rows, width), f32),
+            pltpu.VMEM((nproducts, lanes, 1, rows, 2, nvec), bf16),
+            pltpu.SemaphoreType.DMA((nproducts,)),
+            pltpu.SemaphoreType.DMA,
             pltpu.SemaphoreType.DMA((nelem,)),
             pltpu.SemaphoreType.DMA,
             pltpu.SemaphoreType.DMA((lanes, CAP_LANE)),
@@ -476,6 +505,13 @@
         second_ops,
         product_ops.transpose(0, 1, 3, 2),
     )
+    products = pl.pallas_call(
+        relay,
+        out_shape=jax.ShapeDtypeStruct(products.shape, bf16),
+        in_specs=[anywhere],
+        out_specs=anywhere,
+        scratch_shapes=[pltpu.SemaphoreType.DMA((nproducts,))],
+    )(products)
     return (products, sums.T)
 
 

time: 51.5 us -> 83.8 us (1.63)
  Pallas kernels: 47.1 us -> 82.4 us
  local copies, waits for them, and re-layouts: 3.66 us -> 0.57 us
    pallas_call x0 -> x1, Pallas kernels: none -> 36.9 us  [shards(): pl.pallas_call(relay, out_shape=jax.ShapeDtypeStruct(products.shape, bf16...]
    unnamed x4 -> x3, local copies, waits for them, and re-layouts: 3.66 us -> 0.57 us
    pallas_call x1, Pallas kernels: 47.1 us -> 45.5 us  [shards(): pl.pallas_call(kernel, out_shape=(jax.ShapeDtypeStruct((nproducts, lanes,...]
where the time goes in v3:
time: 83.8 us; the launch traced here: 83.7 us
  Pallas kernels  82.4 us (98%)
    pallas_call x1, Pallas kernels, shards(): pl.pallas_call(kernel, out_shape=(jax.ShapeDtypeStruct((nproducts, lanes,...  45.5 us
    pallas_call x1, Pallas kernels, shards(): pl.pallas_call(relay, out_shape=jax.ShapeDtypeStruct(products.shape, bf16...  36.9 us

profile of v3, /device:TPU:0, one launch (start us, length us, event | category | flops | bytes accessed | tf_op | source)
XLA Modules:
  0.0 83.7 jit_solution(16308489208904379171)
XLA Ops:
  0.6 45.5 %shard_map.104 = (bf16[4,2,1,96,2,384]{5,4,3,2,1,0:T(2,128)(2,1)}, f32[2,8]{1,0:T(2,128)}) custom-call(bf16[4,96,2,384]{3,2,1,0:T(2,128)(2,1)} %refs_0_.1, bf16[4,384,2,384]{3,2,1,0:T(2,128)(2,1)} %refs_1_.1, s32[4,8]{1,0:T(4,128)} %bitcast.3, s32[1,4]{1,0:T(1,128)} %refs_6_.1, s32[1,4]{1,0:T(1,128)} %refs_7_.1, s32[1,4]{1,0:T(1,128)} %refs_5_.1, ...), custom_call_target="tpu_custom_call" | custom-call | tf_op jit(solution)/shard_map/pallas_call | solution.py:441
  46.2 0.0 copy-start
  46.2 36.9 %shard_map.105 = bf16[4,2,1,96,2,384]{5,4,3,2,1,0:T(2,128)(2,1)} custom-call(bf16[4,2,1,96,2,384]{5,4,3,2,1,0:T(2,128)(2,1)} %get-tuple-element.4.source), custom_call_target="tpu_custom_call" | custom-call | tf_op jit(solution)/shard_map/pallas_call | solution.py:508
  83.1 0.0 copy-done
  83.1 0.6 copy.12
Async XLA Ops:
  46.2 36.9 %copy-start = (f32[2,8]{1,0:T(2,128)S(1)}, f32[2,8]{1,0:T(2,128)}, u32[]{:S(2)}) copy-start(f32[2,8]{1,0:T(2,128)} %get-tuple-element.5) | copy-start | bytes 196

commit v4 on v3

--- a/solution.py
+++ b/solution.py
@@ -508,9 +508,10 @@
     products = pl.pallas_call(
         relay,
         out_shape=jax.ShapeDtypeStruct(products.shape, bf16),
-        in_specs=[anywhere],
+        in_specs=[vmem],
         out_specs=anywhere,
         scratch_shapes=[pltpu.SemaphoreType.DMA((nproducts,))],
+        compiler_params=pltpu.CompilerParams(vmem_limit_bytes=58 * 2**20),
     )(products)
     return (products, sums.T)
 

time: 83.8 us -> 49.3 us (0.59)
  Pallas kernels: 82.4 us -> 47.9 us
    pallas_call x1, Pallas kernels: 36.9 us -> 2.31 us  [shards(): pl.pallas_call(relay, out_shape=jax.ShapeDtypeStruct(products.shape, bf16...]
where the time goes in v4:
time: 49.3 us; the launch traced here: 49.1 us
  Pallas kernels  47.9 us (97%)
  between operations  0.66 us (1%)
  local copies, waits for them, and re-layouts  0.57 us (1%)
    pallas_call x1, Pallas kernels, shards(): pl.pallas_call(kernel, out_shape=(jax.ShapeDtypeStruct((nproducts, lanes,...  45.5 us
    pallas_call x1, Pallas kernels, shards(): pl.pallas_call(relay, out_shape=jax.ShapeDtypeStruct(products.shape, bf16...  2.31 us

profile of v4, /device:TPU:0, one launch (start us, length us, event | category | flops | bytes accessed | tf_op | source)
XLA Modules:
  0.0 49.1 jit_solution(6152691595489631766)
XLA Ops:
  0.6 45.5 %shard_map.104 = (bf16[4,2,1,96,2,384]{5,4,3,2,1,0:T(2,128)(2,1)}, f32[2,8]{1,0:T(2,128)}) custom-call(bf16[4,96,2,384]{3,2,1,0:T(2,128)(2,1)} %refs_0_.1, bf16[4,384,2,384]{3,2,1,0:T(2,128)(2,1)} %refs_1_.1, s32[4,8]{1,0:T(4,128)} %bitcast.3, s32[1,4]{1,0:T(1,128)} %refs_6_.1, s32[1,4]{1,0:T(1,128)} %refs_7_.1, s32[1,4]{1,0:T(1,128)} %refs_5_.1, ...), custom_call_target="tpu_custom_call" | custom-call | tf_op jit(solution)/shard_map/pallas_call | solution.py:441
  46.2 0.0 copy-start
  46.2 2.3 %shard_map.105 = bf16[4,2,1,96,2,384]{5,4,3,2,1,0:T(2,128)(2,1)} custom-call(bf16[4,2,1,96,2,384]{5,4,3,2,1,0:T(2,128)(2,1)} %get-tuple-element.4.source), custom_call_target="tpu_custom_call" | custom-call | tf_op jit(solution)/shard_map/pallas_call | solution.py:508
  48.5 0.0 copy-done
  48.5 0.6 %copy.12 = f32[8,2]{0,1:T(2,128)} copy(f32[8,2]{0,1:T(2,128)S(1)} %bitcast.5) | data formatting | bytes 128
Async XLA Ops:
  46.2 2.3 %copy-start = (f32[2,8]{1,0:T(2,128)S(1)}, f32[2,8]{1,0:T(2,128)}, u32[]{:S(2)}) copy-start(f32[2,8]{1,0:T(2,128)} %get-tuple-element.5) | copy-start | bytes 196
